TPU v7x, 128 devices: a whole 4x4x4 slice. The times are simulated.
128 devices in a mesh: row: 8 (over y, core), col: 16 (over z, x).
Axes of the slice: x: 4, y: 4, z: 4, core: 2. Of those that a mesh axis runs over, the one named last changes fastest.
Arguments:
- child_fronts: float32 [20, 512, 20, 1024], P(None, 'col', None, 'row'), as said below
- parent_diagonal: float32 [16384], replicated, may hold values from 0.5 to 4
- block_maps: int32 [2, 20], replicated, may hold values from 0 to 31, as said below
Outputs:
- factored: float32 [16384, 16384], P('row', 'col')
Inputs may be any that keep to these rules, and one draw needn't show every extreme that they name: `child_fronts`: each child's matrix is symmetric and positive definite. `block_maps`: each row names 20 distinct front blocks in increasing order; every one of the 32 front blocks is named by at least one row, and exactly 8 of them by both rows.
All inputs are finite; a program needn't handle non-finite values.
Results may differ from a plain program's by a relative error of at most 0.0001.
Values sent between devices are 32-bit elements; how exact they have to be, the bound alone decides.
No kernel may reach another device: no remote copies, remote signals or barrier semaphores. Data moves between devices by JAX's collectives and lax.ppermute only.
A program may use at most 128 MiB of HBM per device.

v0:
```python
import jax
import jax.numpy as jnp
from jax import lax
from jax.sharding import PartitionSpec as P

B = 512


def broadcast(x, axis, root):
    mine = lax.axis_index(axis) == root
    return lax.psum(jnp.where(mine, x, jnp.zeros_like(x)), axis)


def inverse_maps(block_maps, count):
    blocks = jnp.arange(count, dtype=jnp.int32)
    matches = block_maps[:, None, :] == blocks[None, :, None]
    present = jnp.any(matches, axis=2)
    places = jnp.arange(block_maps.shape[1], dtype=jnp.int32)
    source = jnp.sum(jnp.where(matches, places[None, None, :], 0), axis=2)
    return (source, present)


def shards(child_fronts, parent_diagonal, block_maps):
    row_count = lax.axis_size("row")
    column_count = lax.axis_size("col")
    row_index = lax.axis_index("row")
    column_index = lax.axis_index("col")
    half_count = row_count // 2
    blocks = parent_diagonal.shape[0] // B
    local_rows = blocks // row_count
    local_cols = blocks // column_count
    slice_rows = B // column_count
    slice_cols = 2 * B // row_count
    source, present = inverse_maps(block_maps, blocks)
    my_child = row_index // half_count
    my_source = lax.dynamic_index_in_dim(source, my_child, 0, keepdims=False)
    my_present = lax.dynamic_index_in_dim(present, my_child, 0, keepdims=False)
    picked_rows = jnp.take(child_fronts, my_source, axis=0)
    picked_both = jnp.take(picked_rows, my_source, axis=2)
    keep_mask = my_present[:, None, None, None] & my_present[None, None, :, None]
    picked_both = jnp.where(keep_mask, picked_both, 0.0)
    buffer = picked_both.reshape(
        local_rows, row_count, slice_rows, local_cols, column_count, slice_cols
    )
    buffer = buffer.transpose(1, 4, 0, 2, 3, 5).reshape(row_count * column_count, -1)
    received = lax.all_to_all(buffer, ("row", "col"), split_axis=0, concat_axis=0, tiled=True)
    received = received.reshape(
        2, half_count, column_count, local_rows, slice_rows, local_cols, slice_cols
    )
    summed = received[0] + received[1]
    frontal = summed.transpose(2, 1, 3, 4, 0, 5).reshape(local_rows, B, local_cols, B)
    row_blocks = jnp.arange(local_rows, dtype=jnp.int32) * row_count + row_index
    col_blocks = jnp.arange(local_cols, dtype=jnp.int32) * column_count + column_index
    diag_table = parent_diagonal.reshape(blocks, B)
    diag_rows = jnp.take(diag_table, row_blocks, axis=0)
    same_block = row_blocks[:, None] == col_blocks[None, :]
    identity = jnp.arange(B)[:, None] == jnp.arange(B)[None, :]
    diag_mask = same_block[:, None, :, None] & identity[None, :, None, :]
    frontal = frontal + jnp.where(diag_mask, diag_rows[:, :, None, None], 0.0)
    for panel_index in range(2):
        column_slab = frontal[:, :, panel_index // column_count, :]
        root_row = panel_index % row_count
        local_row = panel_index // row_count
        root_col = panel_index % column_count
        diagonal = broadcast(column_slab[local_row], "row", root_row)
        lower_factor = jnp.linalg.cholesky(diagonal)
        solved = jax.scipy.linalg.solve_triangular(
            lower_factor, column_slab.reshape(-1, B).T, lower=True
        ).T
        solved = solved.reshape(local_rows, B, B)
        factor_factor_column = jnp.where(
            (row_blocks > panel_index)[:, None, None],
            solved,
            jnp.where((row_blocks == panel_index)[:, None, None], lower_factor[None], 0.0),
        )
        factor_factor_column = broadcast(factor_factor_column, "col", root_col)
        owner_rows = (
            jnp.arange(local_cols, dtype=jnp.int32) * column_count + column_index
        ) // row_count
        factor_picked_rows = jnp.take(factor_factor_column, owner_rows, axis=0)
        factor_across = broadcast(factor_picked_rows, "row", column_index % row_count)
        section = frontal
        span_count = local_cols - 0
        product = lax.dot_general(
            factor_factor_column.reshape(-1, B),
            factor_across.reshape(-1, B),
            (((1,), (1,)), ((), ())),
            precision=lax.Precision.HIGHEST,
            preferred_element_type=jnp.float32,
        )
        product = product.reshape(local_rows, B, span_count, B)
        inside = (row_blocks > panel_index)[:, None, None, None] & (col_blocks > panel_index)[
            None, None, :, None
        ]
        section = jnp.where(inside, section - product, section)
        section = jnp.where(
            (col_blocks == panel_index)[None, None, :, None],
            factor_factor_column[:, :, None, :],
            section,
        )
        upper_mask = (row_blocks == panel_index)[:, None, None, None] & (col_blocks > panel_index)[
            None, None, :, None
        ]
        section = jnp.where(upper_mask, 0.0, section)
        frontal = frontal.at[:, :, 0:local_cols, :].set(section)
    return frontal.reshape(local_rows * B, local_cols * B)


def solution(mesh):
    return jax.shard_map(
        shards,
        mesh=mesh,
        in_specs=(P(None, "col", None, "row"), P(), P()),
        out_specs=P("row", "col"),
        check_vma=False,
    )
```

profile of v0, /device:TPU:0, one launch (start us, length us, event | category | flops | bytes accessed | tf_op | source)
XLA Modules:
  0.0 1235.0 jit_solution(6929566411655299351)
XLA Ops:
  15.6 10.1 broadcast_select_fusion
  25.7 12.2 gather_fusion.1
  38.7 29.2 %fusion = f32[4,8,32,2,16,128]{5,3,2,0,4,1:T(2,128)} fusion(f32[4,8,32,2,16,128]{5,2,1,0,4,3:T(8,128)} %bitcast.155, pred[2,16]{0,1:T(8,128)(4,1)S(1)} %copy.53, pred[4,8,2,16]{2,0,3,1:T(4,128)(4,1)S(1)} %broadcast_and_fusion), kind=kLoop, calls=%fused_computation.10 | loop fusion | flops 8388608 | bytes 33555488 | tf_op jit(solution)/shard_map/jit(_where)/select_n | solution.py:41
  67.9 11.7 all-to-all-start
  80.8 231.2 %all-to-all-done = f32[128,1,32768]{2,1,0:T(1,128)} async-done(((f32[128,1,32768]{2,1,0:T(1,128)}), f32[128,1,32768]{2,1,0:T(1,128)}, u32[]{:S(2)}, u32[]{:S(2)}) %all-to-all-start) | async-done | bytes 16777248 | tf_op jit(solution)/shard_map/all_to_all | solution.py:46
  312.0 11.0 slice_add_fusion
  323.0 12.1 copy.56
  335.1 10.3 reshape.505
  345.4 9.9 copy.57
  380.2 59.8 %all-reduce.8.cloned.1.call-done = f32[512,512]{0,1:T(8,128)} async-done(((f32[512,512]{0,1:T(8,128)}), f32[512,512]{0,1:T(8,128)}) %all-reduce.8.cloned.1.call-update) | async-done | bytes 1048592 | tf_op jit(solution)/shard_map/psum | solution.py:11
  443.1 11.7 cholesky.286
  455.0 9.8 custom-call.27
  465.5 11.7 cholesky.305
  477.2 10.0 custom-call.28
  487.9 11.7 cholesky.326
  510.7 11.7 cholesky.343
  534.8 39.3 %custom-call.30 = f32[4,128,128]{1,2,0:T(8,128)S(1)} custom-call(f32[4,128,128]{2,1,0:T(8,128)S(1)} %get-tuple-element.62), custom_call_target="InvertDiagBlocksLowerTriangular" | custom-call | tf_op jit(solution)/shard_map/jit(_solve_triangular)/triangular_solve | solution.py:67
  598.1 102.9 %all-reduce.10.cloned.1.call-done = f32[4,512,512]{2,1,0:T(8,128)} async-done(((f32[4,512,512]{2,1,0:T(8,128)}), f32[4,512,512]{2,1,0:T(8,128)}) %all-reduce.10.cloned.1.call-update) | async-done | bytes 4194320 | tf_op jit(solution)/shard_map/psum | solution.py:11
  711.1 60.1 %all-reduce.12.cloned.1.call-done = f32[2,512,512]{2,1,0:T(8,128)} async-done(((f32[2,512,512]{2,1,0:T(8,128)}), f32[2,512,512]{2,1,0:T(8,128)}) %all-reduce.12.cloned.1.call-update) | async-done | bytes 2097168 | tf_op jit(solution)/shard_map/psum | solution.py:11
  771.2 17.6 %fusion.2 = f32[4,512,2,512]{1,3,2,0:T(8,128)S(1)} fusion(f32[4,512,2,512]{1,3,2,0:T(8,128)} %copy-done, f32[4,512,512]{1,2,0:T(8,128)} %copy.62, pred[2]{0:T(512)(128)(4,1)S(1)} %get-tuple-element.118, pred[4,2]{1,0:T(4,128)(4,1)S(1)} %get-tuple-element.111, pred[4,2]{1,0:T(4,128)(4,1)S(1)} %get-tuple-element.110, ...), kind=kOutput, calls=%fused_computation.14 | convolution fusion | flops 12893290496 | bytes 27262994 | tf_op jit(solution)/shard_map/dot_general | solution.py:84
  808.7 46.8 %all-reduce.14.cloned.1.call-done = f32[512,512]{0,1:T(8,128)} async-done(((f32[512,512]{0,1:T(8,128)}), f32[512,512]{0,1:T(8,128)}) %all-reduce.14.cloned.1.call-update) | async-done | bytes 1048592 | tf_op jit(solution)/shard_map/psum | solution.py:11
  858.5 11.7 cholesky.358
  870.4 9.8 custom-call.31
  880.9 11.7 cholesky.377
  894.0 10.0 custom-call.32
  904.6 11.7 cholesky.398
  927.5 11.7 cholesky.415
  950.9 39.3 %custom-call.34 = f32[4,128,128]{1,2,0:T(8,128)S(1)} custom-call(f32[4,128,128]{2,1,0:T(8,128)S(1)} %get-tuple-element.63), custom_call_target="InvertDiagBlocksLowerTriangular" | custom-call | tf_op jit(solution)/shard_map/jit(_solve_triangular)/triangular_solve | solution.py:67
  1014.3 102.8 %all-reduce.16.cloned.1.call-done = f32[4,512,512]{2,1,0:T(8,128)} async-done(((f32[4,512,512]{2,1,0:T(8,128)}), f32[4,512,512]{2,1,0:T(8,128)}) %all-reduce.16.cloned.1.call-update) | async-done | bytes 4194320 | tf_op jit(solution)/shard_map/psum | solution.py:11
  1127.1 60.2 %all-reduce.18.cloned.1.call-done = f32[2,512,512]{2,1,0:T(8,128)} async-done(((f32[2,512,512]{2,1,0:T(8,128)}), f32[2,512,512]{2,1,0:T(8,128)}) %all-reduce.18.cloned.1.call-update) | async-done | bytes 2097168 | tf_op jit(solution)/shard_map/psum | solution.py:11
  1187.3 18.7 %fusion.4 = f32[4,512,2,512]{1,3,2,0:T(8,128)} fusion(f32[4,512,2,512]{1,3,2,0:T(8,128)} %copy-done.1, f32[4,512,512]{1,2,0:T(8,128)} %copy.68, pred[2]{0:T(512)(128)(4,1)S(1)} %get-tuple-element.124, pred[4,2]{1,0:T(4,128)(4,1)S(1)} %get-tuple-element.109, pred[4,2]{1,0:T(4,128)(4,1)S(1)} %get-tuple-element.108, ...), kind=kOutput, calls=%fused_computation.16 | convolution fusion | flops 12893290496 | bytes 27262994 | tf_op jit(solution)/shard_map/dot_general | solution.py:84
  1205.9 13.2 %copy.70 = f32[4,512,2,512]{3,2,1,0:T(2,128)} copy(f32[4,512,2,512]{1,3,2,0:T(8,128)} %fusion.4) | data formatting | bytes 16777216 | tf_op jit(solution)/shard_map/jit(_where)/select_n | solution.py:104
  (167 shorter events, 199.5 us)
Async XLA Ops:
  67.9 12.0 copy-start.4
  67.9 244.1 %all-to-all-start = ((f32[128,1,32768]{2,1,0:T(1,128)}), f32[128,1,32768]{2,1,0:T(1,128)}, u32[]{:S(2)}, u32[]{:S(2)}) async-start(f32[128,1,32768]{2,1,0:T(1,128)} %bitcast.154), calls=%async_computation | async-start | bytes 33554432 | tf_op jit(solution)/shard_map/all_to_all | solution.py:46
  79.6 360.5 %all-reduce.8.cloned.1.call-start = ((), (), s32[]{:S(2)}) async-start(), calls=%async_computation.1 | async-start | bytes 2097152 | tf_op jit(solution)/shard_map/psum | solution.py:11
  360.0 3.4 copy-start
  364.5 336.6 %all-reduce.10.cloned.1.call-start = ((), (), s32[]{:S(2)}) async-start(), calls=%async_computation.2 | async-start | bytes 8388608 | tf_op jit(solution)/shard_map/psum | solution.py:11
  574.1 5.7 copy-start.2
  598.0 173.1 %all-reduce.12.cloned.1.call-start = ((), (), s32[]{:S(2)}) async-start(), calls=%async_computation.3 | async-start | bytes 4194304 | tf_op jit(solution)/shard_map/psum | solution.py:11
  705.7 149.8 %all-reduce.14.cloned.1.call-start = ((), (), s32[]{:S(2)}) async-start(), calls=%async_computation.4 | async-start | bytes 2097152 | tf_op jit(solution)/shard_map/psum | solution.py:11
  788.8 3.4 copy-start.1
  793.3 323.8 %all-reduce.16.cloned.1.call-start = ((), (), s32[]{:S(2)}) async-start(), calls=%async_computation.5 | async-start | bytes 8388608 | tf_op jit(solution)/shard_map/psum | solution.py:11
  990.2 5.7 copy-start.3
  1014.1 173.1 %all-reduce.18.cloned.1.call-start = ((), (), s32[]{:S(2)}) async-start(), calls=%async_computation.6 | async-start | bytes 4194304 | tf_op jit(solution)/shard_map/psum | solution.py:11
Sparse Core Ops, SparseCore 0:
  364.6 75.4 all-reduce.7
  598.1 102.8 all-reduce.9
  705.8 65.3 all-reduce.11
  793.4 62.0 all-reduce.13
  1014.2 102.8 all-reduce.15
  1121.9 65.3 all-reduce.17
where the time goes:
time: 1240 us; the launch traced here: 1230 us
  waiting for transfers between devices  664 us (54%)
  other arithmetic  317 us (26%)
  local copies, waits for them, and re-layouts  160 us (13%)
  matrix products  62.2 us (5%)
  between operations  19.3 us (2%)
  starting transfers between devices  12.4 us (1%)
    psum x6, waiting for transfers between devices, broadcast(): return lax.psum(jnp.where(mine, x, jnp.zeros_like(x)), axis)  433 us
    all_to_all x1, waiting for transfers between devices, shards(): lax.all_to_all(buffer, ('row', 'col'), split_axis=0, concat_axis=0, tiled...  231 us
    another operation x29, other arithmetic, shards(): lower_factor = jnp.linalg.cholesky(diagonal)  158 us
    another operation x5, other arithmetic, shards(): jax.scipy.linalg.solve_triangular(lower_factor, column_slab.reshape(-1, B...  79.9 us
    dot_general x2, matrix products, shards(): lax.dot_general(factor_factor_column.reshape(-1, B), factor_across.reshap...  36.3 us
    select_n x1, other arithmetic, shards(): picked_both = jnp.where(keep_mask, picked_both, 0.0)  29.2 us
  transfers between devices with their start and end apart: 7, of which 7 were waited for; matrix products, arithmetic and copies ran while one was open for 3% of the time, Pallas kernels for 0%

commit v1 on v0

--- a/solution.py
+++ b/solution.py
@@ -8,7 +8,7 @@
 
 def broadcast(x, axis, root):
     mine = lax.axis_index(axis) == root
-    return lax.psum(jnp.where(mine, x, jnp.zeros_like(x)), axis)
+    return lax.all_gather(jnp.where(mine, x, jnp.zeros_like(x)), axis_name=axis).sum(axis=0)
 
 
 def inverse_maps(block_maps, count):

time: 1240 us -> 1870 us (1.51)
  waiting for transfers between devices: 664 us -> 1220 us
  other arithmetic: 317 us -> 385 us
  matrix products: 62.2 us -> 88.8 us
  local copies, waits for them, and re-layouts: 160 us -> 135 us
    all_gather x0 -> x6, waiting for transfers between devices: none -> 989 us  [broadcast(): lax.all_gather(jnp.where(mine, x, jnp.zeros_like(x)), axis_name=axis)]
    psum x6 -> x0, waiting for transfers between devices: 433 us -> none  [broadcast(): return lax.psum(jnp.where(mine, x, jnp.zeros_like(x)), axis)]
    reduce_sum x0 -> x6, other arithmetic: none -> 71.3 us  [broadcast(): lax.all_gather(jnp.where(mine, x, jnp.zeros_like(x)), axis_name=axis)]
    dot_general x2, matrix products: 36.3 us -> 62.9 us  [shards(): lax.dot_general(factor_factor_column.reshape(-1, B), factor_across.reshap...]
  transfers between devices with their start and end apart: 7 -> 7, of which waited for: 7 -> 7; matrix products, arithmetic and copies ran while one was open for 3% -> 2% of each run, Pallas kernels for 0% -> 0%
where the time goes in v1:
time: 1870 us; the launch traced here: 1860 us
  waiting for transfers between devices  1220 us (65%)
  other arithmetic  385 us (21%)
  local copies, waits for them, and re-layouts  135 us (7%)
  matrix products  88.8 us (5%)
  between operations  19.5 us (1%)
    all_gather x6, waiting for transfers between devices, broadcast(): lax.all_gather(jnp.where(mine, x, jnp.zeros_like(x)), axis_name=axis)  989 us
    all_to_all x1, waiting for transfers between devices, shards(): lax.all_to_all(buffer, ('row', 'col'), split_axis=0, concat_axis=0, tiled...  231 us
    another operation x29, other arithmetic, shards(): lower_factor = jnp.linalg.cholesky(diagonal)  159 us
    another operation x5, other arithmetic, shards(): jax.scipy.linalg.solve_triangular(lower_factor, column_slab.reshape(-1, B...  79.2 us
    reduce_sum x6, other arithmetic, broadcast(): lax.all_gather(jnp.where(mine, x, jnp.zeros_like(x)), axis_name=axis)  71.3 us
    dot_general x2, matrix products, shards(): lax.dot_general(factor_factor_column.reshape(-1, B), factor_across.reshap...  62.9 us
  transfers between devices with their start and end apart: 7, of which 7 were waited for; matrix products, arithmetic and copies ran while one was open for 2% of the time, Pallas kernels for 0%

profile of v1, /device:TPU:0, one launch (start us, length us, event | category | flops | bytes accessed | tf_op | source)
XLA Modules:
  0.0 1860.9 jit_solution(4462616231610715015)
XLA Ops:
  15.6 10.1 broadcast_select_fusion
  25.7 12.2 gather_fusion.1
  38.7 29.2 %fusion = f32[4,8,32,2,16,128]{5,3,2,0,4,1:T(2,128)} fusion(f32[4,8,32,2,16,128]{5,2,1,0,4,3:T(8,128)} %bitcast.141, pred[2,16]{0,1:T(8,128)(4,1)S(1)} %copy.64, pred[4,8,2,16]{2,0,3,1:T(4,128)(4,1)S(1)} %broadcast_and_fusion), kind=kLoop, calls=%fused_computation.10 | loop fusion | flops 8388608 | bytes 33555488 | tf_op jit(solution)/shard_map/jit(_where)/select_n | solution.py:41
  67.9 11.7 all-to-all-start
  81.0 231.0 %all-to-all-done = f32[128,1,32768]{2,1,0:T(1,128)} async-done(((f32[128,1,32768]{2,1,0:T(1,128)}), f32[128,1,32768]{2,1,0:T(1,128)}, u32[]{:S(2)}, u32[]{:S(2)}) %all-to-all-start) | async-done | bytes 16777248 | tf_op jit(solution)/shard_map/all_to_all | solution.py:46
  312.0 11.0 slice_add_fusion
  323.0 12.1 copy.67
  335.1 10.3 reshape.557
  364.3 52.6 %all-gather.15.cloned.1.call-done = f32[8,512,1,512]{3,1,2,0:T(8,128)} async-done(((f32[1,512,1,512]{3,1,2,0:T(8,128)}), f32[8,512,1,512]{3,1,2,0:T(8,128)}) %all-gather.15.cloned.1.call-update) | async-done | bytes 8388624 | tf_op jit(solution)/shard_map/all_gather | solution.py:11
  421.9 11.7 cholesky.286
  433.8 9.8 custom-call.27
  444.3 11.9 cholesky.305
  456.3 9.8 custom-call.28
  466.7 11.7 cholesky.326
  489.6 12.2 cholesky.343
  514.3 39.3 %custom-call.30 = f32[4,128,128]{1,2,0:T(8,128)S(1)} custom-call(f32[4,128,128]{2,1,0:T(8,128)S(1)} %get-tuple-element.62), custom_call_target="InvertDiagBlocksLowerTriangular" | custom-call | tf_op jit(solution)/shard_map/jit(_solve_triangular)/triangular_solve | solution.py:67
  577.8 369.0 %all-gather.11.cloned.1.call-done = f32[16,4,512,512]{3,2,1,0:T(8,128)} async-done(((f32[1,4,512,512]{3,2,1,0:T(8,128)}), f32[16,4,512,512]{3,2,1,0:T(8,128)}) %all-gather.11.cloned.1.call-update) | async-done | bytes 67108880 | tf_op jit(solution)/shard_map/all_gather | solution.py:11
  946.7 23.1 %reduce_sum.65 = f32[4,512,512]{2,1,0:T(8,128)} reduce(f32[16,4,512,512]{3,2,1,0:T(8,128)} %all-gather.11.cloned.1.call-done, f32[]{:T(128)} %constant.284.clone.1), dimensions={0}, to_apply=%region_11.14 | reduce | flops 15728640 | bytes 71303168 | tf_op jit(solution)/shard_map/reduce_sum | solution.py:11
  980.1 79.2 %all-gather.17.cloned.1.call-done = f32[16,512,512]{2,1,0:T(8,128)} async-done(((f32[2,512,512]{2,1,0:T(8,128)}), f32[16,512,512]{2,1,0:T(8,128)}) %all-gather.17.cloned.1.call-update) | async-done | bytes 16777232 | tf_op jit(solution)/shard_map/all_gather | solution.py:11
  1067.3 31.4 %fusion.2 = f32[4,512,2,512]{3,1,2,0:T(8,128)S(1)} fusion(f32[4,512,2,512]{3,1,2,0:T(8,128)} %copy-done.1, f32[4,512,512]{2,1,0:T(8,128)} %reduce_sum.65, pred[2]{0:T(512)(128)(4,1)S(1)} %get-tuple-element.118, pred[4,2]{1,0:T(4,128)(4,1)S(1)} %get-tuple-element.111, pred[4,2]{1,0:T(4,128)(4,1)S(1)} %get-tuple-element.110, ...), kind=kOutput, calls=%fused_computation.14 | convolution fusion | flops 12893290496 | bytes 27262994 | tf_op jit(solution)/shard_map/dot_general | solution.py:84
  1113.7 40.0 %all-gather.19.cloned.1.call-done = f32[8,512,1,512]{3,1,2,0:T(8,128)} async-done(((f32[1,512,1,512]{3,1,2,0:T(8,128)}), f32[8,512,1,512]{3,1,2,0:T(8,128)}) %all-gather.19.cloned.1.call-update) | async-done | bytes 8388624 | tf_op jit(solution)/shard_map/all_gather | solution.py:11
  1158.8 11.7 cholesky.358
  1170.7 9.8 custom-call.31
  1181.2 11.9 cholesky.377
  1204.9 11.7 cholesky.398
  1227.7 12.1 cholesky.415
  1251.6 39.3 %custom-call.34 = f32[4,128,128]{1,2,0:T(8,128)S(1)} custom-call(f32[4,128,128]{2,1,0:T(8,128)S(1)} %get-tuple-element.63), custom_call_target="InvertDiagBlocksLowerTriangular" | custom-call | tf_op jit(solution)/shard_map/jit(_solve_triangular)/triangular_solve | solution.py:67
  1315.0 369.0 %all-gather.13.cloned.1.call-done = f32[16,4,512,512]{3,2,1,0:T(8,128)} async-done(((f32[1,4,512,512]{3,2,1,0:T(8,128)}), f32[16,4,512,512]{3,2,1,0:T(8,128)}) %all-gather.13.cloned.1.call-update) | async-done | bytes 67108880 | tf_op jit(solution)/shard_map/all_gather | solution.py:11
  1684.0 23.1 %reduce_sum.68 = f32[4,512,512]{2,1,0:T(8,128)} reduce(f32[16,4,512,512]{3,2,1,0:T(8,128)} %all-gather.13.cloned.1.call-done, f32[]{:T(128)} %constant.284.clone.1), dimensions={0}, to_apply=%region_14.18 | reduce | flops 15728640 | bytes 71303168 | tf_op jit(solution)/shard_map/reduce_sum | solution.py:11
  1717.3 79.2 %all-gather.21.cloned.1.call-done = f32[16,512,512]{2,1,0:T(8,128)} async-done(((f32[2,512,512]{2,1,0:T(8,128)}), f32[16,512,512]{2,1,0:T(8,128)}) %all-gather.21.cloned.1.call-update) | async-done | bytes 16777232 | tf_op jit(solution)/shard_map/all_gather | solution.py:11
  1804.6 31.4 %fusion.4 = f32[4,512,2,512]{3,1,2,0:T(8,128)S(1)} fusion(f32[4,512,2,512]{3,1,2,0:T(8,128)} %copy-done, f32[4,512,512]{2,1,0:T(8,128)} %reduce_sum.68, pred[2]{0:T(512)(128)(4,1)S(1)} %get-tuple-element.124, pred[4,2]{1,0:T(4,128)(4,1)S(1)} %get-tuple-element.109, pred[4,2]{1,0:T(4,128)(4,1)S(1)} %get-tuple-element.108, f32[4,512,512,1]{1,0,2,3:T(4,128)} %bitcast.144, ...), kind=kOutput, calls=%fused_computation.16 | convolution fusion | flops 12893290496 | bytes 27262994 | tf_op jit(solution)/shard_map/dot_general | solution.py:84
  1836.0 12.4 copy.82
  (170 shorter events, 216.7 us)
Async XLA Ops:
  67.9 12.2 copy-start.4
  67.9 244.1 %all-to-all-start = ((f32[128,1,32768]{2,1,0:T(1,128)}), f32[128,1,32768]{2,1,0:T(1,128)}, u32[]{:S(2)}, u32[]{:S(2)}) async-start(f32[128,1,32768]{2,1,0:T(1,128)} %bitcast.140), calls=%async_computation | async-start | bytes 33554432 | tf_op jit(solution)/shard_map/all_to_all | solution.py:46
  79.6 337.3 %all-gather.15.cloned.1.call-start = ((), (), s32[]{:S(2)}) async-start(), calls=%async_computation.3 | async-start | bytes 9437184 | tf_op jit(solution)/shard_map/all_gather | solution.py:11
  349.5 3.4 copy-start.1
  354.0 592.7 %all-gather.11.cloned.1.call-start = ((), (), s32[]{:S(2)}) async-start(), calls=%async_computation.1 | async-start | bytes 71303168 | tf_op jit(solution)/shard_map/all_gather | solution.py:11
  553.6 5.7 copy-start.2
  577.7 481.6 %all-gather.17.cloned.1.call-start = ((), (), s32[]{:S(2)}) async-start(), calls=%async_computation.4 | async-start | bytes 18874368 | tf_op jit(solution)/shard_map/all_gather | solution.py:11
  974.5 179.2 %all-gather.19.cloned.1.call-start = ((), (), s32[]{:S(2)}) async-start(), calls=%async_computation.5 | async-start | bytes 9437184 | tf_op jit(solution)/shard_map/all_gather | solution.py:11
  1098.8 3.4 copy-start
  1103.3 580.7 %all-gather.13.cloned.1.call-start = ((), (), s32[]{:S(2)}) async-start(), calls=%async_computation.2 | async-start | bytes 71303168 | tf_op jit(solution)/shard_map/all_gather | solution.py:11
  1290.9 5.7 copy-start.3
  1314.9 481.6 %all-gather.21.cloned.1.call-start = ((), (), s32[]{:S(2)}) async-start(), calls=%async_computation.6 | async-start | bytes 18874368 | tf_op jit(solution)/shard_map/all_gather | solution.py:11
Sparse Core Ops, SparseCore 0:
  354.1 62.6 all-gather.14
  577.8 368.9 all-gather.10
  974.6 84.5 all-gather.16
  1103.4 50.3 all-gather.18
  1315.0 368.9 all-gather.12
  1711.9 84.5 all-gather.20
